TPU v7x, 256 devices: a whole 4x4x8 slice. The times are simulated.
256 devices in a mesh: dom: 256 (over x, y, z, core).
Axes of the slice: x: 4, y: 4, z: 8, core: 2. Of those that a mesh axis runs over, the one named last changes fastest.
Arguments:
- x_block: float32 [8, 393216], P(None, 'dom'), may hold values from -18 to 18
- p_block: float32 [8, 393216], P(None, 'dom'), may hold values from -18 to 18
- stiff_elem: float32 [20, 20, 65536], P(None, None, 'dom'), may hold values from -6 to 12.4, as said below
- mass_elem: float32 [20, 20, 65536], P(None, None, 'dom'), may hold values from -0.03 to 0.7, as said below
- node_elem: float32 [10, 10, 65536], P(None, None, 'dom'), may hold values from -1 to 6.1, as said below
- elem_edge: int32 [20, 65536], P(None, 'dom'), may hold values from 0 to 1919, as said below
- elem_node: int32 [10, 65536], P(None, 'dom'), may hold values from 0 to 575, as said below
- send_edge: int32 [6, 16384], P(None, 'dom'), may hold values from 0 to 1535, as said below
- send_node: int32 [6, 8192], P(None, 'dom'), may hold values from 0 to 383, as said below
- grad_pairs: int32 [2, 393216], P(None, 'dom'), may hold values from 0 to 575, as said below
Outputs:
- w_block: float32 [8, 393216], P(None, 'dom')
- gram_stiff: float32 [24, 24], replicated
- gram_mass: float32 [24, 24], replicated
Inputs may be any that keep to these rules, and one draw needn't show every extreme that they name: `stiff_elem`: each element's matrix is symmetric and positive definite. `mass_elem`: each element's matrix is symmetric and positive definite. `node_elem`: each element's matrix is symmetric and positive definite. `elem_edge`: the 20 entries of one element are distinct, and every entry of a subdomain's extended edge list is used by some element of that subdomain. `elem_node`: the 10 entries of one element are distinct, and every entry of a subdomain's extended nodal list is used by some element of that subdomain. `send_edge`: the 64 entries of one direction of one subdomain are distinct. `send_node`: the 32 entries of one direction of one subdomain are distinct. `grad_pairs`: the tail and head of one edge unknown differ.
All inputs are finite; a program needn't handle non-finite values.
Results may differ from a plain program's by a relative error of at most 0.0001.
Values sent between devices are 32-bit elements; how exact they have to be, the bound alone decides.
A program may use at most 128 MiB of HBM per device.

v0:
```python
import jax
import jax.numpy as jnp
from jax import lax
from jax.sharding import PartitionSpec as P

CHEB_DEG = 3
NNODE = 384
highest = lax.Precision.HIGHEST
OFFSETS = (1, -1, 4, -4, 16, -16)
interval_low = 0.3
interval_high = 1.7
jacobi_weight = 0.7


def from_behind(shard, axis, by):
    length = lax.axis_size(axis)
    return lax.ppermute(shard, axis, [(i, (i + by) % length) for i in range(length)])


def edge_extend(values, send_edge):
    pieces = [values]
    for direction in range(6):
        outgoing = values[:, send_edge[direction]]
        pieces.append(from_behind(outgoing, "dom", OFFSETS[direction]))
    return jnp.concatenate(pieces, axis=1)


def edge_return(extended, send_edge):
    ghosts = send_edge.shape[1]
    owned = extended.shape[1] - 6 * ghosts
    total = extended[:, :owned]
    for direction in range(6):
        start = owned + direction * ghosts
        back = from_behind(extended[:, start : start + ghosts], "dom", -OFFSETS[direction])
        total = total.at[:, send_edge[direction]].add(back)
    return total


def node_extend(values, send_node):
    pieces = [values]
    for direction in range(6):
        outgoing = values[:, send_node[direction]]
        pieces.append(from_behind(outgoing, "dom", OFFSETS[direction]))
    return jnp.concatenate(pieces, axis=1)


def node_return(extended, send_node):
    ghosts = send_node.shape[1]
    owned = extended.shape[1] - 6 * ghosts
    total = extended[:, :owned]
    for direction in range(6):
        start = owned + direction * ghosts
        back = from_behind(extended[:, start : start + ghosts], "dom", -OFFSETS[direction])
        total = total.at[:, send_node[direction]].add(back)
    return total


def element_terms(matrices, values):
    return jnp.einsum("jke,cke->cje", matrices, values, precision=highest)


def scatter_local(terms, connect, length):
    return jnp.zeros((terms.shape[0], length), jnp.float32).at[:, connect].add(terms)


def inner_rows(left, right):
    return jnp.einsum("cn,dn->cd", left, right, precision=highest)


def arrange(pair_part, row_part, modes):
    mode_mode = pair_part[:, :modes, :modes]
    mode_prev = pair_part[:, :modes, modes:]
    prev_mode = pair_part[:, modes:, :modes]
    prev_prev = pair_part[:, modes:, modes:]
    new_mode = jnp.swapaxes(row_part[:, :, :modes], 1, 2)
    new_prev = jnp.swapaxes(row_part[:, :, 2 * modes :], 1, 2)
    upper = jnp.concatenate([mode_mode, new_mode, mode_prev], axis=2)
    lower = jnp.concatenate([prev_mode, new_prev, prev_prev], axis=2)
    return jnp.concatenate([upper, row_part, lower], axis=1)


def shards(
    x_block,
    p_block,
    stiff_elem,
    mass_elem,
    node_elem,
    elem_edge,
    elem_node,
    send_edge,
    send_node,
    grad_pairs,
):
    modes = x_block.shape[0]
    owned_edges = x_block.shape[1]
    edge_length = owned_edges + 6 * send_edge.shape[1]
    node_length = NNODE + 6 * send_node.shape[1]
    pair = jnp.concatenate([x_block, p_block], axis=0)
    pair_values = edge_extend(pair, send_edge)[:, elem_edge]
    stiff_pair = element_terms(stiff_elem, pair_values)
    mass_pair = element_terms(mass_elem, pair_values)
    edge_diag = edge_return(
        scatter_local(jnp.einsum("jje->je", stiff_elem)[None], elem_edge, edge_length), send_edge
    )[0]
    node_diag = node_return(
        scatter_local(jnp.einsum("jje->je", node_elem)[None], elem_node, node_length), send_node
    )[0]
    images = edge_return(
        scatter_local(jnp.concatenate([stiff_pair, mass_pair], axis=0), elem_edge, edge_length),
        send_edge,
    )
    stiff_x = images[:modes]
    stiff_p = images[modes : 2 * modes]
    mass_x = images[2 * modes : 3 * modes]
    mass_p = images[3 * modes :]
    numerator, denominator = lax.psum(
        (jnp.sum(x_block * stiff_x, axis=1), jnp.sum(x_block * mass_x, axis=1)), "dom"
    )
    quotient = numerator / denominator
    residual = stiff_x - quotient[:, None] * mass_x

    def stiff_image(vectors):
        values = edge_extend(vectors, send_edge)[:, elem_edge]
        return edge_return(
            scatter_local(element_terms(stiff_elem, values), elem_edge, edge_length), send_edge
        )

    center = 0.5 * (interval_high + interval_low)
    spread = 0.5 * (interval_high - interval_low)
    sigma = center / spread
    rho_now = 1.0 / sigma
    step_dir = residual / (center * edge_diag)
    smooth = step_dir
    for turn in range(CHEB_DEG - 1):
        rho_next = 1.0 / (2.0 * sigma - rho_now)
        remain = residual - stiff_image(smooth)
        step_dir = rho_next * rho_now * step_dir + 2.0 * rho_next / spread * remain / edge_diag
        smooth = smooth + step_dir
        rho_now = rho_next
    after = residual - stiff_image(smooth)
    tails = grad_pairs[0]
    heads = grad_pairs[1]
    gathered_res = (
        jnp.zeros((modes, node_length), jnp.float32)
        .at[:, heads]
        .add(after)
        .at[:, tails]
        .add(-after)
    )
    nodal_res = node_return(gathered_res, send_node)
    first = jacobi_weight * nodal_res / node_diag
    first_values = node_extend(first, send_node)[:, elem_node]
    node_image = node_return(
        scatter_local(element_terms(node_elem, first_values), elem_node, node_length), send_node
    )
    second = first + jacobi_weight * (nodal_res - node_image) / node_diag
    second_full = node_extend(second, send_node)
    w_block = smooth + second_full[:, heads] - second_full[:, tails]
    basis = jnp.concatenate([x_block, w_block, p_block], axis=0)
    w_values = edge_extend(w_block, send_edge)[:, elem_edge]
    stiff_wterm = element_terms(stiff_elem, w_values)
    mass_wterm = element_terms(mass_elem, w_values)
    w_images = edge_return(
        scatter_local(jnp.concatenate([stiff_wterm, mass_wterm], axis=0), elem_edge, edge_length),
        send_edge,
    )
    w_rows = jnp.stack([inner_rows(w_images[:modes], basis), inner_rows(w_images[modes:], basis)])
    stiff_part = inner_rows(pair, jnp.concatenate([stiff_x, stiff_p], axis=0))
    mass_part = inner_rows(pair, jnp.concatenate([mass_x, mass_p], axis=0))
    full_gram = lax.psum(arrange(jnp.stack([stiff_part, mass_part]), w_rows, modes), "dom")
    total_edges = owned_edges * lax.axis_size("dom")
    return (w_block, full_gram[0] / total_edges, full_gram[1] / total_edges)


def solution(mesh):
    in_specs = (
        P(None, "dom"),
        P(None, "dom"),
        P(None, None, "dom"),
        P(None, None, "dom"),
        P(None, None, "dom"),
        P(None, "dom"),
        P(None, "dom"),
        P(None, "dom"),
        P(None, "dom"),
        P(None, "dom"),
    )
    out_specs = (P(None, "dom"), P(), P())
    return jax.shard_map(shards, mesh=mesh, in_specs=in_specs, out_specs=out_specs, check_vma=False)
```

profile of v0, /device:TPU:1, one launch (start us, length us, event | category | flops | bytes accessed | tf_op | source)
XLA Modules:
  0.0 1168.0 jit_solution(15326669690173513750)
XLA Ops:
  13.2 6.9 collective-permute-start.3
  22.1 27.5 %scatter_custom_fusion.7 = f32[1920]{0:T(1024)S(1)} fusion(s32[5120]{0:T(1024)S(1)} %reshape.805, f32[5120]{0:T(1024)S(1)} %reshape.865, f32[]{:T(128)} %constant.12.clone.1), kind=kCustom, calls=%fused_computation.356 | custom fusion | flops 5120 | bytes 7684 | tf_op jit(solution)/shard_map/scatter-add | solution.py:63
  63.1 7.5 collective-permute-start.12
  76.2 18.8 %gather_fusion.6 = f32[5120,16]{1,0:T(8,128)} fusion(f32[16,1920]{0,1:T(8,128)} %constant_dynamic-update-slice_fusion.2, s32[5120]{0:T(1024)S(1)} %broadcast_clamp_fusion), kind=kCustom, calls=%fused_computation.6 | custom fusion | bytes 675840 | tf_op jit(solution)/shard_map/gather | solution.py:99
  98.9 7.3 fusion.7
  108.8 8.9 fusion.4
  125.9 29.0 %scatter_custom_fusion = f32[32,1920]{0,1:T(8,128)} fusion(s32[5120]{0:T(1024)S(1)} %reshape.805, f32[5120,32]{1,0:T(8,128)} %bitcast.336, f32[]{:T(128)} %constant.12.clone.1), kind=kCustom, calls=%fused_computation.162 | custom fusion | flops 163840 | bytes 246272 | tf_op jit(solution)/shard_map/scatter-add | solution.py:63
  160.7 8.8 collective-permute-start.8
  200.7 90.2 %all-reduce = (f32[8]{0:T(128)S(1)}, f32[8]{0:T(128)S(1)}) all-reduce(f32[8]{0:T(128)S(1)} %get-tuple-element.16, f32[8]{0:T(128)S(1)} %get-tuple-element.15), channel_id=1, replica_groups=mesh['dom'=256] {'dom'}, use_global_device_ids=true, to_apply=%region_8.0 | all-reduce | flops 16 | bytes 128 | tf_op jit(solution)/shard_map/psum | solution.py:116
  309.4 7.8 collective-permute-start.21
  325.6 18.8 %gather_fusion.13 = f32[5120,8]{1,0:T(8,128)} fusion(f32[8,1920]{0,1:T(8,128)} %constant_dynamic-update-slice_fusion.9, s32[5120]{0:T(1024)S(1)} %broadcast_clamp_fusion), kind=kCustom, calls=%fused_computation.13 | custom fusion | bytes 348160 | tf_op jit(solution)/shard_map/gather | solution.py:123
  348.2 7.2 convolution_bitcast_fusion.5
  360.9 29.0 %scatter_custom_fusion.14 = f32[8,1920]{0,1:T(8,128)} fusion(s32[5120]{0:T(1024)S(1)} %reshape.805, f32[5120,8]{1,0:T(8,128)} %copy.192, f32[]{:T(128)} %constant.12.clone.1), kind=kCustom, calls=%fused_computation.159 | custom fusion | flops 40960 | bytes 61952 | tf_op jit(solution)/shard_map/scatter-add | solution.py:63
  391.4 8.7 collective-permute-start.24
  407.1 18.2 %scatter_custom_fusion.43 = f32[576]{0:T(1024)S(1)} fusion(s32[2560]{0:T(1024)S(1)} %reshape.1165, f32[2560]{0:T(1024)S(1)} %reshape.1167, f32[]{:T(128)} %constant.12.clone.1), kind=kCustom, calls=%fused_computation.370 | custom fusion | flops 2560 | bytes 2308 | tf_op jit(solution)/shard_map/scatter-add | solution.py:63
  462.2 8.8 collective-permute-start.33
  479.6 18.8 %gather_fusion.20 = f32[5120,8]{1,0:T(8,128)} fusion(f32[8,1920]{0,1:T(8,128)} %constant_dynamic-update-slice_fusion.16, s32[5120]{0:T(1024)S(1)} %broadcast_clamp_fusion), kind=kCustom, calls=%fused_computation.20 | custom fusion | bytes 348160 | tf_op jit(solution)/shard_map/gather | solution.py:123
  502.2 7.2 convolution_bitcast_fusion.4
  513.2 29.0 %scatter_custom_fusion.21 = f32[8,1920]{0,1:T(8,128)} fusion(s32[5120]{0:T(1024)S(1)} %reshape.805, f32[5120,8]{1,0:T(8,128)} %copy.196, f32[]{:T(128)} %constant.12.clone.1), kind=kCustom, calls=%fused_computation.157 | custom fusion | flops 40960 | bytes 61952 | tf_op jit(solution)/shard_map/scatter-add | solution.py:63
  543.1 11.8 %collective-permute-start.36 = (f32[8,64]{0,1:T(8,128)S(1)}, f32[8,64]{0,1:T(8,128)S(1)}, u32[]{:S(2)}, u32[]{:S(2)}) collective-permute-start(f32[8,64]{0,1:T(8,128)S(1)} %get-tuple-element.48), channel_id=1, source_target_pairs={{0,255},{1,0},{2,1},{3,2},{4,3},{5,4},{6,5},{7,6},{8,7},{9,8},{10,... | collective-permute-start | bytes 6152 | tf_op jit(solution)/shard_map/ppermute | solution.py:17
  599.7 9.2 collective-permute-start.45
  609.0 5.2 collective-permute-start.47
  617.8 18.8 %gather_fusion.27 = f32[5120,8]{1,0:T(8,128)} fusion(f32[8,1920]{0,1:T(8,128)} %constant_dynamic-update-slice_fusion.23, s32[5120]{0:T(1024)S(1)} %broadcast_clamp_fusion), kind=kCustom, calls=%fused_computation.27 | custom fusion | bytes 348160 | tf_op jit(solution)/shard_map/gather | solution.py:123
  640.4 7.2 convolution_bitcast_fusion.3
  651.4 29.0 %scatter_custom_fusion.28 = f32[8,1920]{0,1:T(8,128)} fusion(s32[5120]{0:T(1024)S(1)} %reshape.805, f32[5120,8]{1,0:T(8,128)} %copy.200, f32[]{:T(128)} %constant.12.clone.1), kind=kCustom, calls=%fused_computation.155 | custom fusion | flops 40960 | bytes 61952 | tf_op jit(solution)/shard_map/scatter-add | solution.py:63
  681.3 11.9 %collective-permute-start.48 = (f32[8,64]{0,1:T(8,128)S(1)}, f32[8,64]{0,1:T(8,128)S(1)}, u32[]{:S(2)}, u32[]{:S(2)}) collective-permute-start(f32[8,64]{0,1:T(8,128)S(1)} %get-tuple-element.42), channel_id=1, source_target_pairs={{0,255},{1,0},{2,1},{3,2},{4,3},{5,4},{6,5},{7,6},{8,7},{9,8},{10,... | collective-permute-start | bytes 6152 | tf_op jit(solution)/shard_map/ppermute | solution.py:17
  713.3 8.7 collective-permute-start.62
  731.1 9.4 scatter_custom_fusion.35
  740.5 9.4 scatter_custom_fusion.36
  750.5 6.0 collective-permute-start.54
  760.0 10.8 collective-permute-start.56
  795.6 6.9 collective-permute-start.66
  813.0 11.3 collective-permute-start.69
  828.5 5.2 collective-permute-start.71
  834.8 5.6 gather_fusion.34
  844.2 6.3 convolution_bitcast_fusion.2
  853.6 14.6 %scatter_custom_fusion.50 = f32[8,576]{0,1:T(8,128)S(1)} fusion(s32[2560]{0:T(1024)S(1)} %reshape.1165, f32[2560,8]{1,0:T(8,128)} %copy.204, f32[]{:T(128)} %constant.12.clone.1), kind=kCustom, calls=%fused_computation.172 | custom fusion | flops 20480 | bytes 18944 | tf_op jit(solution)/shard_map/scatter-add | solution.py:63
  868.2 11.6 collective-permute-start.72
  882.2 5.3 collective-permute-start.76
  920.8 7.8 collective-permute-start.81
  947.2 5.7 collective-permute-start.84
  966.3 7.0 collective-permute-start.85
  973.3 7.8 collective-permute-start.87
  989.7 18.8 %gather_fusion.49 = f32[5120,8]{1,0:T(8,128)} fusion(f32[8,1920]{0,1:T(8,128)} %constant_dynamic-update-slice_fusion.44, s32[5120]{0:T(1024)S(1)} %copy-done.10), kind=kCustom, calls=%fused_computation.49 | custom fusion | bytes 348160 | tf_op jit(solution)/shard_map/gather | solution.py:160
  1012.3 7.3 convolution_bitcast_fusion.1
  1027.7 28.6 %scatter_custom_fusion.57 = f32[16,1920]{0,1:T(8,128)S(1)} fusion(s32[5120]{0:T(1024)} %copy-done.16, f32[5120,16]{1,0:T(8,128)} %bitcast.335, f32[]{:T(128)} %constant.12.clone.1), kind=kCustom, calls=%fused_computation.153 | custom fusion | flops 81920 | bytes 123392 | tf_op jit(solution)/shard_map/scatter-add | solution.py:63
  1056.3 8.3 collective-permute-start.90
  1084.6 82.3 %psum.23 = f32[2,24,24]{2,1,0:T(8,128)S(1)} all-reduce(f32[2,24,24]{2,1,0:T(8,128)S(1)} %fusion.101), channel_id=1, replica_groups=mesh['dom'=256] {'dom'}, use_global_device_ids=true, to_apply=%region_70.0 | all-reduce | flops 1152 | bytes 9216 | tf_op jit(solution)/shard_map/psum | solution.py:170
  (516 shorter events, 429.5 us)
Async XLA Ops:
  4.7 52.9 %collective-permute-start = (f32[16,64]{0,1:T(8,128)}, f32[16,64]{0,1:T(8,128)S(1)}, u32[]{:S(2)}, u32[]{:S(2)}) collective-permute-start(f32[16,64]{0,1:T(8,128)} %bitcast.2), channel_id=1, source_target_pairs={{0,1},{1,2},{2,3},{3,4},{4,5},{5,6},{6,7},{7,8},{8,9},{9,10},{10,1... | collective-permute-start | bytes 12296 | tf_op jit(solution)/shard_map/ppermute | solution.py:17
  9.0 54.1 %collective-permute-start.1 = (f32[16,64]{0,1:T(8,128)}, f32[16,64]{0,1:T(8,128)S(1)}, u32[]{:S(2)}, u32[]{:S(2)}) collective-permute-start(f32[16,64]{0,1:T(8,128)} %bitcast.5), channel_id=1, source_target_pairs={{0,255},{1,0},{2,1},{3,2},{4,3},{5,4},{6,5},{7,6},{8,7},{9,8},{10,... | collective-permute-start | bytes 12296 | tf_op jit(solution)/shard_map/ppermute | solution.py:17
  9.8 61.4 %collective-permute-start.2 = (f32[16,64]{0,1:T(8,128)S(1)}, f32[16,64]{0,1:T(8,128)S(1)}, u32[]{:S(2)}, u32[]{:S(2)}) collective-permute-start(f32[16,64]{0,1:T(8,128)S(1)} %bitcast.344), channel_id=1, source_target_pairs={{0,4},{1,5},{2,6},{3,7},{4,8},{5,9},{6,10},{7,11},{8,12},{9,13},{1... | collective-permute-start | bytes 12296 | tf_op jit(solution)/shard_map/ppermute | solution.py:17
  13.2 58.5 %collective-permute-start.3 = (f32[16,64]{0,1:T(8,128)S(1)}, f32[16,64]{0,1:T(8,128)S(1)}, u32[]{:S(2)}, u32[]{:S(2)}) collective-permute-start(f32[16,64]{0,1:T(8,128)S(1)} %bitcast.343), channel_id=1, source_target_pairs={{0,252},{1,253},{2,254},{3,255},{4,0},{5,1},{6,2},{7,3},{8,4},{9,5... | collective-permute-start | bytes 12296 | tf_op jit(solution)/shard_map/ppermute | solution.py:17
  20.7 51.6 %collective-permute-start.4 = (f32[16,64]{0,1:T(8,128)S(1)}, f32[16,64]{0,1:T(8,128)S(1)}, u32[]{:S(2)}, u32[]{:S(2)}) collective-permute-start(f32[16,64]{0,1:T(8,128)S(1)} %bitcast.342), channel_id=1, source_target_pairs={{0,16},{1,17},{2,18},{3,19},{4,20},{5,21},{6,22},{7,23},{8,24},{9,... | collective-permute-start | bytes 12296 | tf_op jit(solution)/shard_map/ppermute | solution.py:17
  57.7 17.9 %collective-permute-start.5 = (f32[16,64]{0,1:T(8,128)}, f32[16,64]{0,1:T(8,128)S(1)}, u32[]{:S(2)}, u32[]{:S(2)}) collective-permute-start(f32[16,64]{0,1:T(8,128)} %bitcast.345), channel_id=1, source_target_pairs={{0,240},{1,241},{2,242},{3,243},{4,244},{5,245},{6,246},{7,247},{8... | collective-permute-start | bytes 12296 | tf_op jit(solution)/shard_map/ppermute | solution.py:17
  63.1 94.9 %collective-permute-start.12 = (f32[1,64]{1,0:T(1,128)}, f32[1,64]{1,0:T(1,128)}, u32[]{:S(2)}, u32[]{:S(2)}) collective-permute-start(f32[1,64]{1,0:T(1,128)} %get-tuple-element.87), channel_id=1, source_target_pairs={{0,255},{1,0},{2,1},{3,2},{4,3},{5,4},{6,5},{7,6},{8,7},{9,8},{10,... | collective-permute-start | bytes 776 | tf_op jit(solution)/shard_map/ppermute | solution.py:17
  71.2 87.3 %collective-permute-start.13 = (f32[1,64]{1,0:T(1,128)}, f32[1,64]{1,0:T(1,128)}, u32[]{:S(2)}, u32[]{:S(2)}) collective-permute-start(f32[1,64]{1,0:T(1,128)} %get-tuple-element.86), channel_id=1, source_target_pairs={{0,1},{1,2},{2,3},{3,4},{4,5},{5,6},{6,7},{7,8},{8,9},{9,10},{10,1... | collective-permute-start | bytes 776 | tf_op jit(solution)/shard_map/ppermute | solution.py:17
  71.8 87.7 %collective-permute-start.14 = (f32[1,64]{1,0:T(1,128)}, f32[1,64]{1,0:T(1,128)}, u32[]{:S(2)}, u32[]{:S(2)}) collective-permute-start(f32[1,64]{1,0:T(1,128)} %get-tuple-element.85), channel_id=1, source_target_pairs={{0,252},{1,253},{2,254},{3,255},{4,0},{5,1},{6,2},{7,3},{8,4},{9,5... | collective-permute-start | bytes 776 | tf_op jit(solution)/shard_map/ppermute | solution.py:17
  72.4 88.3 %collective-permute-start.15 = (f32[1,64]{1,0:T(1,128)}, f32[1,64]{1,0:T(1,128)}, u32[]{:S(2)}, u32[]{:S(2)}) collective-permute-start(f32[1,64]{1,0:T(1,128)} %get-tuple-element.84), channel_id=1, source_target_pairs={{0,4},{1,5},{2,6},{3,7},{4,8},{5,9},{6,10},{7,11},{8,12},{9,13},{1... | collective-permute-start | bytes 776 | tf_op jit(solution)/shard_map/ppermute | solution.py:17
  159.5 24.2 %collective-permute-start.7 = (f32[32,64]{0,1:T(8,128)S(1)}, f32[32,64]{0,1:T(8,128)S(1)}, u32[]{:S(2)}, u32[]{:S(2)}) collective-permute-start(f32[32,64]{0,1:T(8,128)S(1)} %get-tuple-element.59), channel_id=1, source_target_pairs={{0,1},{1,2},{2,3},{3,4},{4,5},{5,6},{6,7},{7,8},{8,9},{9,10},{10,1... | collective-permute-start | bytes 24584 | tf_op jit(solution)/shard_map/ppermute | solution.py:17
  160.7 25.9 %collective-permute-start.8 = (f32[32,64]{0,1:T(8,128)S(1)}, f32[32,64]{0,1:T(8,128)}, u32[]{:S(2)}, u32[]{:S(2)}) collective-permute-start(f32[32,64]{0,1:T(8,128)S(1)} %get-tuple-element.58), channel_id=1, source_target_pairs={{0,252},{1,253},{2,254},{3,255},{4,0},{5,1},{6,2},{7,3},{8,4},{9,5... | collective-permute-start | bytes 24584 | tf_op jit(solution)/shard_map/ppermute | solution.py:17
  169.5 20.2 %collective-permute-start.9 = (f32[32,64]{0,1:T(8,128)S(1)}, f32[32,64]{0,1:T(8,128)}, u32[]{:S(2)}, u32[]{:S(2)}) collective-permute-start(f32[32,64]{0,1:T(8,128)S(1)} %get-tuple-element.57), channel_id=1, source_target_pairs={{0,4},{1,5},{2,6},{3,7},{4,8},{5,9},{6,10},{7,11},{8,12},{9,13},{1... | collective-permute-start | bytes 24584 | tf_op jit(solution)/shard_map/ppermute | solution.py:17
  169.5 23.3 %collective-permute-start.10 = (f32[32,64]{0,1:T(8,128)S(1)}, f32[32,64]{0,1:T(8,128)}, u32[]{:S(2)}, u32[]{:S(2)}) collective-permute-start(f32[32,64]{0,1:T(8,128)S(1)} %get-tuple-element.56), channel_id=1, source_target_pairs={{0,240},{1,241},{2,242},{3,243},{4,244},{5,245},{6,246},{7,247},{8... | collective-permute-start | bytes 24584 | tf_op jit(solution)/shard_map/ppermute | solution.py:17
  170.0 25.9 %collective-permute-start.11 = (f32[32,64]{0,1:T(8,128)S(1)}, f32[32,64]{0,1:T(8,128)S(1)}, u32[]{:S(2)}, u32[]{:S(2)}) collective-permute-start(f32[32,64]{0,1:T(8,128)S(1)} %get-tuple-element.55), channel_id=1, source_target_pairs={{0,16},{1,17},{2,18},{3,19},{4,20},{5,21},{6,22},{7,23},{8,24},{9,... | collective-permute-start | bytes 24584 | tf_op jit(solution)/shard_map/ppermute | solution.py:17
  295.7 21.5 %collective-permute-start.18 = (f32[8,64]{0,1:T(8,128)S(1)}, f32[8,64]{0,1:T(8,128)S(1)}, u32[]{:S(2)}, u32[]{:S(2)}) collective-permute-start(f32[8,64]{0,1:T(8,128)S(1)} %bitcast.370), channel_id=1, source_target_pairs={{0,1},{1,2},{2,3},{3,4},{4,5},{5,6},{6,7},{7,8},{8,9},{9,10},{10,1... | collective-permute-start | bytes 6152 | tf_op jit(solution)/shard_map/ppermute | solution.py:17
  400.0 30.5 %collective-permute-start.25 = (f32[8,64]{0,1:T(8,128)}, f32[8,64]{0,1:T(8,128)}, u32[]{:S(2)}, u32[]{:S(2)}) collective-permute-start(f32[8,64]{0,1:T(8,128)} %get-tuple-element.53), channel_id=1, source_target_pairs={{0,1},{1,2},{2,3},{3,4},{4,5},{5,6},{6,7},{7,8},{8,9},{9,10},{10,1... | collective-permute-start | bytes 6152 | tf_op jit(solution)/shard_map/ppermute | solution.py:17
  400.0 33.6 %collective-permute-start.26 = (f32[8,64]{0,1:T(8,128)}, f32[8,64]{0,1:T(8,128)}, u32[]{:S(2)}, u32[]{:S(2)}) collective-permute-start(f32[8,64]{0,1:T(8,128)} %get-tuple-element.52), channel_id=1, source_target_pairs={{0,252},{1,253},{2,254},{3,255},{4,0},{5,1},{6,2},{7,3},{8,4},{9,5... | collective-permute-start | bytes 6152 | tf_op jit(solution)/shard_map/ppermute | solution.py:17
  403.0 33.7 %collective-permute-start.27 = (f32[8,64]{0,1:T(8,128)S(1)}, f32[8,64]{0,1:T(8,128)}, u32[]{:S(2)}, u32[]{:S(2)}) collective-permute-start(f32[8,64]{0,1:T(8,128)S(1)} %get-tuple-element.51), channel_id=1, source_target_pairs={{0,4},{1,5},{2,6},{3,7},{4,8},{5,9},{6,10},{7,11},{8,12},{9,13},{1... | collective-permute-start | bytes 6152 | tf_op jit(solution)/shard_map/ppermute | solution.py:17
  403.0 36.8 %collective-permute-start.28 = (f32[8,64]{0,1:T(8,128)S(1)}, f32[8,64]{0,1:T(8,128)}, u32[]{:S(2)}, u32[]{:S(2)}) collective-permute-start(f32[8,64]{0,1:T(8,128)S(1)} %get-tuple-element.50), channel_id=1, source_target_pairs={{0,240},{1,241},{2,242},{3,243},{4,244},{5,245},{6,246},{7,247},{8... | collective-permute-start | bytes 6152 | tf_op jit(solution)/shard_map/ppermute | solution.py:17
  406.4 36.5 %collective-permute-start.29 = (f32[8,64]{0,1:T(8,128)S(1)}, f32[8,64]{0,1:T(8,128)}, u32[]{:S(2)}, u32[]{:S(2)}) collective-permute-start(f32[8,64]{0,1:T(8,128)S(1)} %get-tuple-element.49), channel_id=1, source_target_pairs={{0,16},{1,17},{2,18},{3,19},{4,20},{5,21},{6,22},{7,23},{8,24},{9,... | collective-permute-start | bytes 6152 | tf_op jit(solution)/shard_map/ppermute | solution.py:17
  450.5 20.4 %collective-permute-start.30 = (f32[8,64]{0,1:T(8,128)S(1)}, f32[8,64]{0,1:T(8,128)S(1)}, u32[]{:S(2)}, u32[]{:S(2)}) collective-permute-start(f32[8,64]{0,1:T(8,128)S(1)} %bitcast.367), channel_id=1, source_target_pairs={{0,1},{1,2},{2,3},{3,4},{4,5},{5,6},{6,7},{7,8},{8,9},{9,10},{10,1... | collective-permute-start | bytes 6152 | tf_op jit(solution)/shard_map/ppermute | solution.py:17
  543.1 18.7 %collective-permute-start.36 = (f32[8,64]{0,1:T(8,128)S(1)}, f32[8,64]{0,1:T(8,128)S(1)}, u32[]{:S(2)}, u32[]{:S(2)}) collective-permute-start(f32[8,64]{0,1:T(8,128)S(1)} %get-tuple-element.48), channel_id=1, source_target_pairs={{0,255},{1,0},{2,1},{3,2},{4,3},{5,4},{6,5},{7,6},{8,7},{9,8},{10,... | collective-permute-start | bytes 6152 | tf_op jit(solution)/shard_map/ppermute | solution.py:17
  558.2 18.5 %collective-permute-start.40 = (f32[8,64]{0,1:T(8,128)S(1)}, f32[8,64]{0,1:T(8,128)S(1)}, u32[]{:S(2)}, u32[]{:S(2)}) collective-permute-start(f32[8,64]{0,1:T(8,128)S(1)} %get-tuple-element.44), channel_id=1, source_target_pairs={{0,240},{1,241},{2,242},{3,243},{4,244},{5,245},{6,246},{7,247},{8... | collective-permute-start | bytes 6152 | tf_op jit(solution)/shard_map/ppermute | solution.py:17
  562.4 17.2 %collective-permute-start.41 = (f32[8,64]{0,1:T(8,128)S(1)}, f32[8,64]{0,1:T(8,128)S(1)}, u32[]{:S(2)}, u32[]{:S(2)}) collective-permute-start(f32[8,64]{0,1:T(8,128)S(1)} %get-tuple-element.43), channel_id=1, source_target_pairs={{0,16},{1,17},{2,18},{3,19},{4,20},{5,21},{6,22},{7,23},{8,24},{9,... | collective-permute-start | bytes 6152 | tf_op jit(solution)/shard_map/ppermute | solution.py:17
  588.4 20.5 %collective-permute-start.42 = (f32[8,64]{0,1:T(8,128)}, f32[8,64]{0,1:T(8,128)S(1)}, u32[]{:S(2)}, u32[]{:S(2)}) collective-permute-start(f32[8,64]{0,1:T(8,128)} %bitcast.69), channel_id=1, source_target_pairs={{0,1},{1,2},{2,3},{3,4},{4,5},{5,6},{6,7},{7,8},{8,9},{9,10},{10,1... | collective-permute-start | bytes 6152 | tf_op jit(solution)/shard_map/ppermute | solution.py:17
  681.3 18.8 %collective-permute-start.48 = (f32[8,64]{0,1:T(8,128)S(1)}, f32[8,64]{0,1:T(8,128)S(1)}, u32[]{:S(2)}, u32[]{:S(2)}) collective-permute-start(f32[8,64]{0,1:T(8,128)S(1)} %get-tuple-element.42), channel_id=1, source_target_pairs={{0,255},{1,0},{2,1},{3,2},{4,3},{5,4},{6,5},{7,6},{8,7},{9,8},{10,... | collective-permute-start | bytes 6152 | tf_op jit(solution)/shard_map/ppermute | solution.py:17
  696.2 17.1 %collective-permute-start.51 = (f32[8,64]{0,1:T(8,128)S(1)}, f32[8,64]{0,1:T(8,128)S(1)}, u32[]{:S(2)}, u32[]{:S(2)}) collective-permute-start(f32[8,64]{0,1:T(8,128)S(1)} %get-tuple-element.39), channel_id=1, source_target_pairs={{0,4},{1,5},{2,6},{3,7},{4,8},{5,9},{6,10},{7,11},{8,12},{9,13},{1... | collective-permute-start | bytes 6152 | tf_op jit(solution)/shard_map/ppermute | solution.py:17
  696.2 28.8 %collective-permute-start.52 = (f32[8,64]{0,1:T(8,128)S(1)}, f32[8,64]{0,1:T(8,128)S(1)}, u32[]{:S(2)}, u32[]{:S(2)}) collective-permute-start(f32[8,64]{0,1:T(8,128)S(1)} %get-tuple-element.38), channel_id=1, source_target_pairs={{0,240},{1,241},{2,242},{3,243},{4,244},{5,245},{6,246},{7,247},{8... | collective-permute-start | bytes 6152 | tf_op jit(solution)/shard_map/ppermute | solution.py:17
  700.1 27.9 %collective-permute-start.53 = (f32[8,64]{0,1:T(8,128)S(1)}, f32[8,64]{0,1:T(8,128)S(1)}, u32[]{:S(2)}, u32[]{:S(2)}) collective-permute-start(f32[8,64]{0,1:T(8,128)S(1)} %get-tuple-element.37), channel_id=1, source_target_pairs={{0,16},{1,17},{2,18},{3,19},{4,20},{5,21},{6,22},{7,23},{8,24},{9,... | collective-permute-start | bytes 6152 | tf_op jit(solution)/shard_map/ppermute | solution.py:17
  705.5 51.0 %collective-permute-start.60 = (f32[1,32]{1,0:T(1,128)}, f32[1,32]{1,0:T(1,128)}, u32[]{:S(2)}, u32[]{:S(2)}) collective-permute-start(f32[1,32]{1,0:T(1,128)} %get-tuple-element.105), channel_id=1, source_target_pairs={{0,255},{1,0},{2,1},{3,2},{4,3},{5,4},{6,5},{7,6},{8,7},{9,8},{10,... | collective-permute-start | bytes 392 | tf_op jit(solution)/shard_map/ppermute | solution.py:17
  709.9 47.6 %collective-permute-start.61 = (f32[1,32]{1,0:T(1,128)}, f32[1,32]{1,0:T(1,128)}, u32[]{:S(2)}, u32[]{:S(2)}) collective-permute-start(f32[1,32]{1,0:T(1,128)} %get-tuple-element.104), channel_id=1, source_target_pairs={{0,1},{1,2},{2,3},{3,4},{4,5},{5,6},{6,7},{7,8},{8,9},{9,10},{10,1... | collective-permute-start | bytes 392 | tf_op jit(solution)/shard_map/ppermute | solution.py:17
  713.3 46.6 %collective-permute-start.62 = (f32[1,32]{1,0:T(1,128)}, f32[1,32]{1,0:T(1,128)}, u32[]{:S(2)}, u32[]{:S(2)}) collective-permute-start(f32[1,32]{1,0:T(1,128)} %get-tuple-element.103), channel_id=1, source_target_pairs={{0,252},{1,253},{2,254},{3,255},{4,0},{5,1},{6,2},{7,3},{8,4},{9,5... | collective-permute-start | bytes 392 | tf_op jit(solution)/shard_map/ppermute | solution.py:17
  725.0 34.9 %collective-permute-start.63 = (f32[1,32]{1,0:T(1,128)}, f32[1,32]{1,0:T(1,128)}, u32[]{:S(2)}, u32[]{:S(2)}) collective-permute-start(f32[1,32]{1,0:T(1,128)} %get-tuple-element.102), channel_id=1, source_target_pairs={{0,4},{1,5},{2,6},{3,7},{4,8},{5,9},{6,10},{7,11},{8,12},{9,13},{1... | collective-permute-start | bytes 392 | tf_op jit(solution)/shard_map/ppermute | solution.py:17
  750.5 20.3 %collective-permute-start.54 = (f32[8,32]{0,1:T(8,128)}, f32[8,32]{0,1:T(8,128)}, u32[]{:S(2)}, u32[]{:S(2)}) collective-permute-start(f32[8,32]{0,1:T(8,128)} %get-tuple-element.72), channel_id=1, source_target_pairs={{0,255},{1,0},{2,1},{3,2},{4,3},{5,4},{6,5},{7,6},{8,7},{9,8},{10,... | collective-permute-start | bytes 3080 | tf_op jit(solution)/shard_map/ppermute | solution.py:17
  759.9 19.3 %collective-permute-start.55 = (f32[8,32]{0,1:T(8,128)}, f32[8,32]{0,1:T(8,128)}, u32[]{:S(2)}, u32[]{:S(2)}) collective-permute-start(f32[8,32]{0,1:T(8,128)} %get-tuple-element.71), channel_id=1, source_target_pairs={{0,1},{1,2},{2,3},{3,4},{4,5},{5,6},{6,7},{7,8},{8,9},{9,10},{10,1... | collective-permute-start | bytes 3080 | tf_op jit(solution)/shard_map/ppermute | solution.py:17
  760.0 21.7 %collective-permute-start.56 = (f32[8,32]{0,1:T(8,128)S(1)}, f32[8,32]{0,1:T(8,128)}, u32[]{:S(2)}, u32[]{:S(2)}) collective-permute-start(f32[8,32]{0,1:T(8,128)S(1)} %get-tuple-element.70), channel_id=1, source_target_pairs={{0,252},{1,253},{2,254},{3,255},{4,0},{5,1},{6,2},{7,3},{8,4},{9,5... | collective-permute-start | bytes 3080 | tf_op jit(solution)/shard_map/ppermute | solution.py:17
  770.9 18.2 %collective-permute-start.59 = (f32[8,32]{0,1:T(8,128)S(1)}, f32[8,32]{0,1:T(8,128)}, u32[]{:S(2)}, u32[]{:S(2)}) collective-permute-start(f32[8,32]{0,1:T(8,128)S(1)} %get-tuple-element.67), channel_id=1, source_target_pairs={{0,16},{1,17},{2,18},{3,19},{4,20},{5,21},{6,22},{7,23},{8,24},{9,... | collective-permute-start | bytes 3080 | tf_op jit(solution)/shard_map/ppermute | solution.py:17
  795.6 32.9 %collective-permute-start.66 = (f32[8,32]{0,1:T(8,128)}, f32[8,32]{0,1:T(8,128)S(1)}, u32[]{:S(2)}, u32[]{:S(2)}) collective-permute-start(f32[8,32]{0,1:T(8,128)} %bitcast.112), channel_id=1, source_target_pairs={{0,1},{1,2},{2,3},{3,4},{4,5},{5,6},{6,7},{7,8},{8,9},{9,10},{10,1... | collective-permute-start | bytes 3080 | tf_op jit(solution)/shard_map/ppermute | solution.py:17
  808.6 25.1 %collective-permute-start.67 = (f32[8,32]{0,1:T(8,128)}, f32[8,32]{0,1:T(8,128)}, u32[]{:S(2)}, u32[]{:S(2)}) collective-permute-start(f32[8,32]{0,1:T(8,128)} %bitcast.113), channel_id=1, source_target_pairs={{0,255},{1,0},{2,1},{3,2},{4,3},{5,4},{6,5},{7,6},{8,7},{9,8},{10,... | collective-permute-start | bytes 3080 | tf_op jit(solution)/shard_map/ppermute | solution.py:17
  810.8 23.6 %collective-permute-start.68 = (f32[8,32]{0,1:T(8,128)}, f32[8,32]{0,1:T(8,128)S(1)}, u32[]{:S(2)}, u32[]{:S(2)}) collective-permute-start(f32[8,32]{0,1:T(8,128)} %bitcast.114), channel_id=1, source_target_pairs={{0,4},{1,5},{2,6},{3,7},{4,8},{5,9},{6,10},{7,11},{8,12},{9,13},{1... | collective-permute-start | bytes 3080 | tf_op jit(solution)/shard_map/ppermute | solution.py:17
  813.0 21.4 %collective-permute-start.69 = (f32[8,32]{0,1:T(8,128)}, f32[8,32]{0,1:T(8,128)S(1)}, u32[]{:S(2)}, u32[]{:S(2)}) collective-permute-start(f32[8,32]{0,1:T(8,128)} %bitcast.115), channel_id=1, source_target_pairs={{0,252},{1,253},{2,254},{3,255},{4,0},{5,1},{6,2},{7,3},{8,4},{9,5... | collective-permute-start | bytes 3080 | tf_op jit(solution)/shard_map/ppermute | solution.py:17
  868.2 19.3 %collective-permute-start.72 = (f32[8,32]{0,1:T(8,128)S(1)}, f32[8,32]{0,1:T(8,128)S(1)}, u32[]{:S(2)}, u32[]{:S(2)}) collective-permute-start(f32[8,32]{0,1:T(8,128)S(1)} %get-tuple-element.66), channel_id=1, source_target_pairs={{0,255},{1,0},{2,1},{3,2},{4,3},{5,4},{6,5},{7,6},{8,7},{9,8},{10,... | collective-permute-start | bytes 3080 | tf_op jit(solution)/shard_map/ppermute | solution.py:17
  879.9 16.4 %collective-permute-start.75 = (f32[8,32]{0,1:T(8,128)S(1)}, f32[8,32]{0,1:T(8,128)}, u32[]{:S(2)}, u32[]{:S(2)}) collective-permute-start(f32[8,32]{0,1:T(8,128)S(1)} %get-tuple-element.63), channel_id=1, source_target_pairs={{0,4},{1,5},{2,6},{3,7},{4,8},{5,9},{6,10},{7,11},{8,12},{9,13},{1... | collective-permute-start | bytes 3080 | tf_op jit(solution)/shard_map/ppermute | solution.py:17
  882.2 16.5 %collective-permute-start.76 = (f32[8,32]{0,1:T(8,128)S(1)}, f32[8,32]{0,1:T(8,128)}, u32[]{:S(2)}, u32[]{:S(2)}) collective-permute-start(f32[8,32]{0,1:T(8,128)S(1)} %get-tuple-element.62), channel_id=1, source_target_pairs={{0,240},{1,241},{2,242},{3,243},{4,244},{5,245},{6,246},{7,247},{8... | collective-permute-start | bytes 3080 | tf_op jit(solution)/shard_map/ppermute | solution.py:17
  907.9 20.7 %collective-permute-start.78 = (f32[8,32]{0,1:T(8,128)}, f32[8,32]{0,1:T(8,128)}, u32[]{:S(2)}, u32[]{:S(2)}) collective-permute-start(f32[8,32]{0,1:T(8,128)} %bitcast.128), channel_id=1, source_target_pairs={{0,1},{1,2},{2,3},{3,4},{4,5},{5,6},{6,7},{7,8},{8,9},{9,10},{10,1... | collective-permute-start | bytes 3080 | tf_op jit(solution)/shard_map/ppermute | solution.py:17
  947.2 33.9 %collective-permute-start.84 = (f32[8,64]{0,1:T(8,128)S(1)}, f32[8,64]{0,1:T(8,128)S(1)}, u32[]{:S(2)}, u32[]{:S(2)}) collective-permute-start(f32[8,64]{0,1:T(8,128)S(1)} %bitcast.369), channel_id=1, source_target_pairs={{0,1},{1,2},{2,3},{3,4},{4,5},{5,6},{6,7},{7,8},{8,9},{9,10},{10,1... | collective-permute-start | bytes 6152 | tf_op jit(solution)/shard_map/ppermute | solution.py:17
  966.3 20.4 %collective-permute-start.85 = (f32[8,64]{0,1:T(8,128)}, f32[8,64]{0,1:T(8,128)S(1)}, u32[]{:S(2)}, u32[]{:S(2)}) collective-permute-start(f32[8,64]{0,1:T(8,128)} %bitcast.139), channel_id=1, source_target_pairs={{0,255},{1,0},{2,1},{3,2},{4,3},{5,4},{6,5},{7,6},{8,7},{9,8},{10,... | collective-permute-start | bytes 6152 | tf_op jit(solution)/shard_map/ppermute | solution.py:17
  (105 other events, 5205.4 us)
where the time goes:
time: 1180 us; the launch traced here: 1170 us
  other arithmetic  374 us (32%)
  local copies, waits for them, and re-layouts  290 us (25%)
  starting transfers between devices  266 us (23%)
  blocking collectives  173 us (15%)
  matrix products  61.6 us (5%)
    ppermute x96, starting transfers between devices, from_behind(): lax.ppermute(shard, axis, [(i, (i + by) % length) for i in range(length)])  266 us
    scatter-add x8, other arithmetic, scatter_local(): jnp.zeros((terms.shape[0], length), jnp.float32).at[:, connect].add(terms)  205 us
    psum x1, blocking collectives, shards(): lax.psum((jnp.sum(x_block * stiff_x, axis=1), jnp.sum(x_block * mass_x, a...  90.2 us
    scatter-add x36, other arithmetic, edge_return(): total = total.at[:, send_edge[direction]].add(back)  87 us
    psum x1, blocking collectives, shards(): lax.psum(arrange(jnp.stack([stiff_part, mass_part]), w_rows, modes), 'dom')  82.3 us
    gather x6, local copies, waits for them, and re-layouts, stiff_image(): values = edge_extend(vectors, send_edge)[:, elem_edge]  67.8 us
    dot_general x8, matrix products, element_terms(): return jnp.einsum('jke,cke->cje', matrices, values, precision=highest)  56.3 us
    gather x30, local copies, waits for them, and re-layouts, edge_extend(): outgoing = values[:, send_edge[direction]]  54.6 us
  transfers between devices with their start and end apart: 96, of which 3 were waited for; matrix products, arithmetic and copies ran while one was open for 31% of the time, Pallas kernels for 0%

commit v1 on v0

--- a/solution.py
+++ b/solution.py
@@ -167,7 +167,9 @@
     w_rows = jnp.stack([inner_rows(w_images[:modes], basis), inner_rows(w_images[modes:], basis)])
     stiff_part = inner_rows(pair, jnp.concatenate([stiff_x, stiff_p], axis=0))
     mass_part = inner_rows(pair, jnp.concatenate([mass_x, mass_p], axis=0))
-    full_gram = lax.psum(arrange(jnp.stack([stiff_part, mass_part]), w_rows, modes), "dom")
+    full_gram = jnp.sum(
+        lax.all_gather(arrange(jnp.stack([stiff_part, mass_part]), w_rows, modes), "dom"), axis=0
+    )
     total_edges = owned_edges * lax.axis_size("dom")
     return (w_block, full_gram[0] / total_edges, full_gram[1] / total_edges)
 

time: 1180 us -> 1240 us (1.051)
  waiting for transfers between devices: 2.27 us -> 121 us
  blocking collectives: 173 us -> 90.3 us
  between operations: 2.21 us -> 15.6 us
    all_gather x0 -> x1, waiting for transfers between devices: none -> 119 us  [shards(): lax.all_gather(arrange(jnp.stack([stiff_part, mass_part]), w_rows, modes)...]
    psum x1 -> x0, blocking collectives: 82.3 us -> none  [shards(): lax.psum(arrange(jnp.stack([stiff_part, mass_part]), w_rows, modes), 'dom')]
  transfers between devices with their start and end apart: 96 -> 97, of which waited for: 3 -> 4; matrix products, arithmetic and copies ran while one was open for 31% -> 30% of each run, Pallas kernels for 0% -> 0%
where the time goes in v1:
time: 1240 us; the launch traced here: 1220 us
  other arithmetic  378 us (30%)
  local copies, waits for them, and re-layouts  290 us (23%)
  starting transfers between devices  266 us (21%)
  waiting for transfers between devices  121 us (10%)
  blocking collectives  90.3 us (7%)
  matrix products  61.6 us (5%)
  between operations  15.6 us (1%)
    ppermute x96, starting transfers between devices, from_behind(): lax.ppermute(shard, axis, [(i, (i + by) % length) for i in range(length)])  266 us
    scatter-add x8, other arithmetic, scatter_local(): jnp.zeros((terms.shape[0], length), jnp.float32).at[:, connect].add(terms)  205 us
    all_gather x1, waiting for transfers between devices, shards(): lax.all_gather(arrange(jnp.stack([stiff_part, mass_part]), w_rows, modes)...  119 us
    psum x1, blocking collectives, shards(): lax.psum((jnp.sum(x_block * stiff_x, axis=1), jnp.sum(x_block * mass_x, a...  90.3 us
    scatter-add x36, other arithmetic, edge_return(): total = total.at[:, send_edge[direction]].add(back)  87 us
    gather x6, local copies, waits for them, and re-layouts, stiff_image(): values = edge_extend(vectors, send_edge)[:, elem_edge]  67.8 us
    dot_general x8, matrix products, element_terms(): return jnp.einsum('jke,cke->cje', matrices, values, precision=highest)  56.3 us
    gather x30, local copies, waits for them, and re-layouts, edge_extend(): outgoing = values[:, send_edge[direction]]  54.6 us
  transfers between devices with their start and end apart: 97, of which 4 were waited for; matrix products, arithmetic and copies ran while one was open for 30% of the time, Pallas kernels for 0%

profile of v1, /device:TPU:1, one launch (start us, length us, event | category | flops | bytes accessed | tf_op | source)
XLA Modules:
  0.0 1221.8 jit_solution(2092807653618534598)
XLA Ops:
  19.8 6.9 collective-permute-start.3
  28.6 27.5 %scatter_custom_fusion.7 = f32[1920]{0:T(1024)S(1)} fusion(s32[5120]{0:T(1024)S(1)} %reshape.805, f32[5120]{0:T(1024)S(1)} %reshape.865, f32[]{:T(128)} %constant.12.clone.1), kind=kCustom, calls=%fused_computation.356 | custom fusion | flops 5120 | bytes 7684 | tf_op jit(solution)/shard_map/scatter-add | solution.py:63
  69.7 7.5 collective-permute-start.12
  82.7 18.8 %gather_fusion.6 = f32[5120,16]{1,0:T(8,128)} fusion(f32[16,1920]{0,1:T(8,128)} %constant_dynamic-update-slice_fusion.2, s32[5120]{0:T(1024)S(1)} %broadcast_clamp_fusion), kind=kCustom, calls=%fused_computation.6 | custom fusion | bytes 675840 | tf_op jit(solution)/shard_map/gather | solution.py:99
  105.5 7.3 fusion.7
  115.4 8.9 fusion.4
  132.4 29.0 %scatter_custom_fusion = f32[32,1920]{0,1:T(8,128)} fusion(s32[5120]{0:T(1024)S(1)} %reshape.805, f32[5120,32]{1,0:T(8,128)} %bitcast.338, f32[]{:T(128)} %constant.12.clone.1), kind=kCustom, calls=%fused_computation.162 | custom fusion | flops 163840 | bytes 246272 | tf_op jit(solution)/shard_map/scatter-add | solution.py:63
  167.3 8.8 collective-permute-start.8
  207.3 90.3 %all-reduce = (f32[8]{0:T(128)S(1)}, f32[8]{0:T(128)S(1)}) all-reduce(f32[8]{0:T(128)S(1)} %get-tuple-element.16, f32[8]{0:T(128)S(1)} %get-tuple-element.15), channel_id=1, replica_groups=mesh['dom'=256] {'dom'}, use_global_device_ids=true, to_apply=%region_8.0 | all-reduce | flops 16 | bytes 128 | tf_op jit(solution)/shard_map/psum | solution.py:116
  316.0 7.8 collective-permute-start.21
  332.2 18.8 %gather_fusion.13 = f32[5120,8]{1,0:T(8,128)} fusion(f32[8,1920]{0,1:T(8,128)} %constant_dynamic-update-slice_fusion.9, s32[5120]{0:T(1024)S(1)} %broadcast_clamp_fusion), kind=kCustom, calls=%fused_computation.13 | custom fusion | bytes 348160 | tf_op jit(solution)/shard_map/gather | solution.py:123
  354.8 7.2 convolution_bitcast_fusion.5
  367.4 29.0 %scatter_custom_fusion.14 = f32[8,1920]{0,1:T(8,128)} fusion(s32[5120]{0:T(1024)S(1)} %reshape.805, f32[5120,8]{1,0:T(8,128)} %copy.192, f32[]{:T(128)} %constant.12.clone.1), kind=kCustom, calls=%fused_computation.159 | custom fusion | flops 40960 | bytes 61952 | tf_op jit(solution)/shard_map/scatter-add | solution.py:63
  397.9 8.7 collective-permute-start.24
  413.7 18.2 %scatter_custom_fusion.43 = f32[576]{0:T(1024)S(1)} fusion(s32[2560]{0:T(1024)S(1)} %reshape.1165, f32[2560]{0:T(1024)S(1)} %reshape.1167, f32[]{:T(128)} %constant.12.clone.1), kind=kCustom, calls=%fused_computation.370 | custom fusion | flops 2560 | bytes 2308 | tf_op jit(solution)/shard_map/scatter-add | solution.py:63
  468.7 8.8 collective-permute-start.33
  486.2 18.8 %gather_fusion.20 = f32[5120,8]{1,0:T(8,128)} fusion(f32[8,1920]{0,1:T(8,128)} %constant_dynamic-update-slice_fusion.16, s32[5120]{0:T(1024)S(1)} %broadcast_clamp_fusion), kind=kCustom, calls=%fused_computation.20 | custom fusion | bytes 348160 | tf_op jit(solution)/shard_map/gather | solution.py:123
  508.8 7.2 convolution_bitcast_fusion.4
  519.8 29.0 %scatter_custom_fusion.21 = f32[8,1920]{0,1:T(8,128)} fusion(s32[5120]{0:T(1024)S(1)} %reshape.805, f32[5120,8]{1,0:T(8,128)} %copy.196, f32[]{:T(128)} %constant.12.clone.1), kind=kCustom, calls=%fused_computation.157 | custom fusion | flops 40960 | bytes 61952 | tf_op jit(solution)/shard_map/scatter-add | solution.py:63
  549.7 11.8 collective-permute-start.36
  606.3 9.2 collective-permute-start.45
  615.5 5.2 collective-permute-start.47
  624.4 18.8 %gather_fusion.27 = f32[5120,8]{1,0:T(8,128)} fusion(f32[8,1920]{0,1:T(8,128)} %constant_dynamic-update-slice_fusion.23, s32[5120]{0:T(1024)S(1)} %broadcast_clamp_fusion), kind=kCustom, calls=%fused_computation.27 | custom fusion | bytes 348160 | tf_op jit(solution)/shard_map/gather | solution.py:123
  646.9 7.2 convolution_bitcast_fusion.3
  658.0 29.0 %scatter_custom_fusion.28 = f32[8,1920]{0,1:T(8,128)} fusion(s32[5120]{0:T(1024)S(1)} %reshape.805, f32[5120,8]{1,0:T(8,128)} %copy.200, f32[]{:T(128)} %constant.12.clone.1), kind=kCustom, calls=%fused_computation.155 | custom fusion | flops 40960 | bytes 61952 | tf_op jit(solution)/shard_map/scatter-add | solution.py:63
  687.9 11.9 collective-permute-start.48
  719.9 8.7 collective-permute-start.62
  737.7 9.4 scatter_custom_fusion.35
  747.1 9.4 scatter_custom_fusion.36
  757.1 6.0 collective-permute-start.54
  766.6 10.8 collective-permute-start.56
  802.1 6.9 collective-permute-start.66
  819.6 11.3 collective-permute-start.69
  835.1 5.2 collective-permute-start.71
  841.3 5.6 gather_fusion.34
  850.8 6.3 convolution_bitcast_fusion.2
  860.2 14.6 %scatter_custom_fusion.50 = f32[8,576]{0,1:T(8,128)S(1)} fusion(s32[2560]{0:T(1024)S(1)} %reshape.1165, f32[2560,8]{1,0:T(8,128)} %copy.204, f32[]{:T(128)} %constant.12.clone.1), kind=kCustom, calls=%fused_computation.172 | custom fusion | flops 20480 | bytes 18944 | tf_op jit(solution)/shard_map/scatter-add | solution.py:63
  874.8 11.6 collective-permute-start.72
  888.8 5.3 collective-permute-start.76
  927.4 7.8 collective-permute-start.81
  953.8 5.7 collective-permute-start.84
  972.9 7.0 collective-permute-start.85
  979.9 7.8 collective-permute-start.87
  996.3 18.8 %gather_fusion.49 = f32[5120,8]{1,0:T(8,128)} fusion(f32[8,1920]{0,1:T(8,128)} %constant_dynamic-update-slice_fusion.44, s32[5120]{0:T(1024)S(1)} %copy-done.10), kind=kCustom, calls=%fused_computation.49 | custom fusion | bytes 348160 | tf_op jit(solution)/shard_map/gather | solution.py:160
  1018.9 7.3 convolution_bitcast_fusion.1
  1034.3 28.6 %scatter_custom_fusion.57 = f32[16,1920]{0,1:T(8,128)S(1)} fusion(s32[5120]{0:T(1024)} %copy-done.16, f32[5120,16]{1,0:T(8,128)} %bitcast.337, f32[]{:T(128)} %constant.12.clone.1), kind=kCustom, calls=%fused_computation.153 | custom fusion | flops 81920 | bytes 123392 | tf_op jit(solution)/shard_map/scatter-add | solution.py:63
  1062.9 8.3 collective-permute-start.90
  1091.8 118.8 %all-gather.3.cloned.1.call-done = f32[512,24,24]{2,1,0:T(8,128)} async-done(((f32[2,24,24]{2,1,0:T(8,128)}), f32[512,24,24]{2,1,0:T(8,128)}) %all-gather.3.cloned.1.call-update) | async-done | bytes 1179664 | tf_op jit(solution)/shard_map/all_gather | solution.py:171
  (519 shorter events, 433.5 us)
Async XLA Ops:
  7.2 1203.4 %all-gather.3.cloned.1.call-start = ((), (), s32[]{:S(2)}) async-start(), calls=%async_computation | async-start | bytes 6316032 | tf_op jit(solution)/shard_map/all_gather | solution.py:171
  11.3 52.9 %collective-permute-start = (f32[16,64]{0,1:T(8,128)}, f32[16,64]{0,1:T(8,128)S(1)}, u32[]{:S(2)}, u32[]{:S(2)}) collective-permute-start(f32[16,64]{0,1:T(8,128)} %bitcast.2), channel_id=1, source_target_pairs={{0,1},{1,2},{2,3},{3,4},{4,5},{5,6},{6,7},{7,8},{8,9},{9,10},{10,1... | collective-permute-start | bytes 12296 | tf_op jit(solution)/shard_map/ppermute | solution.py:17
  15.5 54.1 %collective-permute-start.1 = (f32[16,64]{0,1:T(8,128)}, f32[16,64]{0,1:T(8,128)S(1)}, u32[]{:S(2)}, u32[]{:S(2)}) collective-permute-start(f32[16,64]{0,1:T(8,128)} %bitcast.5), channel_id=1, source_target_pairs={{0,255},{1,0},{2,1},{3,2},{4,3},{5,4},{6,5},{7,6},{8,7},{9,8},{10,... | collective-permute-start | bytes 12296 | tf_op jit(solution)/shard_map/ppermute | solution.py:17
  16.4 61.4 %collective-permute-start.2 = (f32[16,64]{0,1:T(8,128)S(1)}, f32[16,64]{0,1:T(8,128)S(1)}, u32[]{:S(2)}, u32[]{:S(2)}) collective-permute-start(f32[16,64]{0,1:T(8,128)S(1)} %bitcast.346), channel_id=1, source_target_pairs={{0,4},{1,5},{2,6},{3,7},{4,8},{5,9},{6,10},{7,11},{8,12},{9,13},{1... | collective-permute-start | bytes 12296 | tf_op jit(solution)/shard_map/ppermute | solution.py:17
  19.8 58.5 %collective-permute-start.3 = (f32[16,64]{0,1:T(8,128)S(1)}, f32[16,64]{0,1:T(8,128)S(1)}, u32[]{:S(2)}, u32[]{:S(2)}) collective-permute-start(f32[16,64]{0,1:T(8,128)S(1)} %bitcast.345), channel_id=1, source_target_pairs={{0,252},{1,253},{2,254},{3,255},{4,0},{5,1},{6,2},{7,3},{8,4},{9,5... | collective-permute-start | bytes 12296 | tf_op jit(solution)/shard_map/ppermute | solution.py:17
  27.3 51.6 %collective-permute-start.4 = (f32[16,64]{0,1:T(8,128)S(1)}, f32[16,64]{0,1:T(8,128)S(1)}, u32[]{:S(2)}, u32[]{:S(2)}) collective-permute-start(f32[16,64]{0,1:T(8,128)S(1)} %bitcast.344), channel_id=1, source_target_pairs={{0,16},{1,17},{2,18},{3,19},{4,20},{5,21},{6,22},{7,23},{8,24},{9,... | collective-permute-start | bytes 12296 | tf_op jit(solution)/shard_map/ppermute | solution.py:17
  64.3 17.9 %collective-permute-start.5 = (f32[16,64]{0,1:T(8,128)}, f32[16,64]{0,1:T(8,128)S(1)}, u32[]{:S(2)}, u32[]{:S(2)}) collective-permute-start(f32[16,64]{0,1:T(8,128)} %bitcast.347), channel_id=1, source_target_pairs={{0,240},{1,241},{2,242},{3,243},{4,244},{5,245},{6,246},{7,247},{8... | collective-permute-start | bytes 12296 | tf_op jit(solution)/shard_map/ppermute | solution.py:17
  69.7 94.9 %collective-permute-start.12 = (f32[1,64]{1,0:T(1,128)}, f32[1,64]{1,0:T(1,128)}, u32[]{:S(2)}, u32[]{:S(2)}) collective-permute-start(f32[1,64]{1,0:T(1,128)} %get-tuple-element.87), channel_id=1, source_target_pairs={{0,255},{1,0},{2,1},{3,2},{4,3},{5,4},{6,5},{7,6},{8,7},{9,8},{10,... | collective-permute-start | bytes 776 | tf_op jit(solution)/shard_map/ppermute | solution.py:17
  77.7 87.3 %collective-permute-start.13 = (f32[1,64]{1,0:T(1,128)}, f32[1,64]{1,0:T(1,128)}, u32[]{:S(2)}, u32[]{:S(2)}) collective-permute-start(f32[1,64]{1,0:T(1,128)} %get-tuple-element.86), channel_id=1, source_target_pairs={{0,1},{1,2},{2,3},{3,4},{4,5},{5,6},{6,7},{7,8},{8,9},{9,10},{10,1... | collective-permute-start | bytes 776 | tf_op jit(solution)/shard_map/ppermute | solution.py:17
  78.4 87.7 %collective-permute-start.14 = (f32[1,64]{1,0:T(1,128)}, f32[1,64]{1,0:T(1,128)}, u32[]{:S(2)}, u32[]{:S(2)}) collective-permute-start(f32[1,64]{1,0:T(1,128)} %get-tuple-element.85), channel_id=1, source_target_pairs={{0,252},{1,253},{2,254},{3,255},{4,0},{5,1},{6,2},{7,3},{8,4},{9,5... | collective-permute-start | bytes 776 | tf_op jit(solution)/shard_map/ppermute | solution.py:17
  79.0 88.3 %collective-permute-start.15 = (f32[1,64]{1,0:T(1,128)}, f32[1,64]{1,0:T(1,128)}, u32[]{:S(2)}, u32[]{:S(2)}) collective-permute-start(f32[1,64]{1,0:T(1,128)} %get-tuple-element.84), channel_id=1, source_target_pairs={{0,4},{1,5},{2,6},{3,7},{4,8},{5,9},{6,10},{7,11},{8,12},{9,13},{1... | collective-permute-start | bytes 776 | tf_op jit(solution)/shard_map/ppermute | solution.py:17
  166.1 24.2 %collective-permute-start.7 = (f32[32,64]{0,1:T(8,128)S(1)}, f32[32,64]{0,1:T(8,128)S(1)}, u32[]{:S(2)}, u32[]{:S(2)}) collective-permute-start(f32[32,64]{0,1:T(8,128)S(1)} %get-tuple-element.59), channel_id=1, source_target_pairs={{0,1},{1,2},{2,3},{3,4},{4,5},{5,6},{6,7},{7,8},{8,9},{9,10},{10,1... | collective-permute-start | bytes 24584 | tf_op jit(solution)/shard_map/ppermute | solution.py:17
  167.3 25.9 %collective-permute-start.8 = (f32[32,64]{0,1:T(8,128)S(1)}, f32[32,64]{0,1:T(8,128)}, u32[]{:S(2)}, u32[]{:S(2)}) collective-permute-start(f32[32,64]{0,1:T(8,128)S(1)} %get-tuple-element.58), channel_id=1, source_target_pairs={{0,252},{1,253},{2,254},{3,255},{4,0},{5,1},{6,2},{7,3},{8,4},{9,5... | collective-permute-start | bytes 24584 | tf_op jit(solution)/shard_map/ppermute | solution.py:17
  176.1 20.2 %collective-permute-start.9 = (f32[32,64]{0,1:T(8,128)S(1)}, f32[32,64]{0,1:T(8,128)}, u32[]{:S(2)}, u32[]{:S(2)}) collective-permute-start(f32[32,64]{0,1:T(8,128)S(1)} %get-tuple-element.57), channel_id=1, source_target_pairs={{0,4},{1,5},{2,6},{3,7},{4,8},{5,9},{6,10},{7,11},{8,12},{9,13},{1... | collective-permute-start | bytes 24584 | tf_op jit(solution)/shard_map/ppermute | solution.py:17
  176.1 23.3 %collective-permute-start.10 = (f32[32,64]{0,1:T(8,128)S(1)}, f32[32,64]{0,1:T(8,128)}, u32[]{:S(2)}, u32[]{:S(2)}) collective-permute-start(f32[32,64]{0,1:T(8,128)S(1)} %get-tuple-element.56), channel_id=1, source_target_pairs={{0,240},{1,241},{2,242},{3,243},{4,244},{5,245},{6,246},{7,247},{8... | collective-permute-start | bytes 24584 | tf_op jit(solution)/shard_map/ppermute | solution.py:17
  176.6 25.9 %collective-permute-start.11 = (f32[32,64]{0,1:T(8,128)S(1)}, f32[32,64]{0,1:T(8,128)S(1)}, u32[]{:S(2)}, u32[]{:S(2)}) collective-permute-start(f32[32,64]{0,1:T(8,128)S(1)} %get-tuple-element.55), channel_id=1, source_target_pairs={{0,16},{1,17},{2,18},{3,19},{4,20},{5,21},{6,22},{7,23},{8,24},{9,... | collective-permute-start | bytes 24584 | tf_op jit(solution)/shard_map/ppermute | solution.py:17
  302.2 21.5 %collective-permute-start.18 = (f32[8,64]{0,1:T(8,128)S(1)}, f32[8,64]{0,1:T(8,128)S(1)}, u32[]{:S(2)}, u32[]{:S(2)}) collective-permute-start(f32[8,64]{0,1:T(8,128)S(1)} %bitcast.372), channel_id=1, source_target_pairs={{0,1},{1,2},{2,3},{3,4},{4,5},{5,6},{6,7},{7,8},{8,9},{9,10},{10,1... | collective-permute-start | bytes 6152 | tf_op jit(solution)/shard_map/ppermute | solution.py:17
  406.6 30.5 %collective-permute-start.25 = (f32[8,64]{0,1:T(8,128)}, f32[8,64]{0,1:T(8,128)}, u32[]{:S(2)}, u32[]{:S(2)}) collective-permute-start(f32[8,64]{0,1:T(8,128)} %get-tuple-element.53), channel_id=1, source_target_pairs={{0,1},{1,2},{2,3},{3,4},{4,5},{5,6},{6,7},{7,8},{8,9},{9,10},{10,1... | collective-permute-start | bytes 6152 | tf_op jit(solution)/shard_map/ppermute | solution.py:17
  406.6 33.6 %collective-permute-start.26 = (f32[8,64]{0,1:T(8,128)}, f32[8,64]{0,1:T(8,128)}, u32[]{:S(2)}, u32[]{:S(2)}) collective-permute-start(f32[8,64]{0,1:T(8,128)} %get-tuple-element.52), channel_id=1, source_target_pairs={{0,252},{1,253},{2,254},{3,255},{4,0},{5,1},{6,2},{7,3},{8,4},{9,5... | collective-permute-start | bytes 6152 | tf_op jit(solution)/shard_map/ppermute | solution.py:17
  409.5 33.7 %collective-permute-start.27 = (f32[8,64]{0,1:T(8,128)S(1)}, f32[8,64]{0,1:T(8,128)}, u32[]{:S(2)}, u32[]{:S(2)}) collective-permute-start(f32[8,64]{0,1:T(8,128)S(1)} %get-tuple-element.51), channel_id=1, source_target_pairs={{0,4},{1,5},{2,6},{3,7},{4,8},{5,9},{6,10},{7,11},{8,12},{9,13},{1... | collective-permute-start | bytes 6152 | tf_op jit(solution)/shard_map/ppermute | solution.py:17
  409.6 36.8 %collective-permute-start.28 = (f32[8,64]{0,1:T(8,128)S(1)}, f32[8,64]{0,1:T(8,128)}, u32[]{:S(2)}, u32[]{:S(2)}) collective-permute-start(f32[8,64]{0,1:T(8,128)S(1)} %get-tuple-element.50), channel_id=1, source_target_pairs={{0,240},{1,241},{2,242},{3,243},{4,244},{5,245},{6,246},{7,247},{8... | collective-permute-start | bytes 6152 | tf_op jit(solution)/shard_map/ppermute | solution.py:17
  413.0 36.5 %collective-permute-start.29 = (f32[8,64]{0,1:T(8,128)S(1)}, f32[8,64]{0,1:T(8,128)}, u32[]{:S(2)}, u32[]{:S(2)}) collective-permute-start(f32[8,64]{0,1:T(8,128)S(1)} %get-tuple-element.49), channel_id=1, source_target_pairs={{0,16},{1,17},{2,18},{3,19},{4,20},{5,21},{6,22},{7,23},{8,24},{9,... | collective-permute-start | bytes 6152 | tf_op jit(solution)/shard_map/ppermute | solution.py:17
  457.1 20.4 %collective-permute-start.30 = (f32[8,64]{0,1:T(8,128)S(1)}, f32[8,64]{0,1:T(8,128)S(1)}, u32[]{:S(2)}, u32[]{:S(2)}) collective-permute-start(f32[8,64]{0,1:T(8,128)S(1)} %bitcast.369), channel_id=1, source_target_pairs={{0,1},{1,2},{2,3},{3,4},{4,5},{5,6},{6,7},{7,8},{8,9},{9,10},{10,1... | collective-permute-start | bytes 6152 | tf_op jit(solution)/shard_map/ppermute | solution.py:17
  549.7 18.7 %collective-permute-start.36 = (f32[8,64]{0,1:T(8,128)S(1)}, f32[8,64]{0,1:T(8,128)S(1)}, u32[]{:S(2)}, u32[]{:S(2)}) collective-permute-start(f32[8,64]{0,1:T(8,128)S(1)} %get-tuple-element.48), channel_id=1, source_target_pairs={{0,255},{1,0},{2,1},{3,2},{4,3},{5,4},{6,5},{7,6},{8,7},{9,8},{10,... | collective-permute-start | bytes 6152 | tf_op jit(solution)/shard_map/ppermute | solution.py:17
  564.8 18.5 %collective-permute-start.40 = (f32[8,64]{0,1:T(8,128)S(1)}, f32[8,64]{0,1:T(8,128)S(1)}, u32[]{:S(2)}, u32[]{:S(2)}) collective-permute-start(f32[8,64]{0,1:T(8,128)S(1)} %get-tuple-element.44), channel_id=1, source_target_pairs={{0,240},{1,241},{2,242},{3,243},{4,244},{5,245},{6,246},{7,247},{8... | collective-permute-start | bytes 6152 | tf_op jit(solution)/shard_map/ppermute | solution.py:17
  569.0 17.2 %collective-permute-start.41 = (f32[8,64]{0,1:T(8,128)S(1)}, f32[8,64]{0,1:T(8,128)S(1)}, u32[]{:S(2)}, u32[]{:S(2)}) collective-permute-start(f32[8,64]{0,1:T(8,128)S(1)} %get-tuple-element.43), channel_id=1, source_target_pairs={{0,16},{1,17},{2,18},{3,19},{4,20},{5,21},{6,22},{7,23},{8,24},{9,... | collective-permute-start | bytes 6152 | tf_op jit(solution)/shard_map/ppermute | solution.py:17
  595.0 20.5 %collective-permute-start.42 = (f32[8,64]{0,1:T(8,128)}, f32[8,64]{0,1:T(8,128)S(1)}, u32[]{:S(2)}, u32[]{:S(2)}) collective-permute-start(f32[8,64]{0,1:T(8,128)} %bitcast.69), channel_id=1, source_target_pairs={{0,1},{1,2},{2,3},{3,4},{4,5},{5,6},{6,7},{7,8},{8,9},{9,10},{10,1... | collective-permute-start | bytes 6152 | tf_op jit(solution)/shard_map/ppermute | solution.py:17
  687.9 18.8 %collective-permute-start.48 = (f32[8,64]{0,1:T(8,128)S(1)}, f32[8,64]{0,1:T(8,128)S(1)}, u32[]{:S(2)}, u32[]{:S(2)}) collective-permute-start(f32[8,64]{0,1:T(8,128)S(1)} %get-tuple-element.42), channel_id=1, source_target_pairs={{0,255},{1,0},{2,1},{3,2},{4,3},{5,4},{6,5},{7,6},{8,7},{9,8},{10,... | collective-permute-start | bytes 6152 | tf_op jit(solution)/shard_map/ppermute | solution.py:17
  702.8 17.1 %collective-permute-start.51 = (f32[8,64]{0,1:T(8,128)S(1)}, f32[8,64]{0,1:T(8,128)S(1)}, u32[]{:S(2)}, u32[]{:S(2)}) collective-permute-start(f32[8,64]{0,1:T(8,128)S(1)} %get-tuple-element.39), channel_id=1, source_target_pairs={{0,4},{1,5},{2,6},{3,7},{4,8},{5,9},{6,10},{7,11},{8,12},{9,13},{1... | collective-permute-start | bytes 6152 | tf_op jit(solution)/shard_map/ppermute | solution.py:17
  702.8 28.8 %collective-permute-start.52 = (f32[8,64]{0,1:T(8,128)S(1)}, f32[8,64]{0,1:T(8,128)S(1)}, u32[]{:S(2)}, u32[]{:S(2)}) collective-permute-start(f32[8,64]{0,1:T(8,128)S(1)} %get-tuple-element.38), channel_id=1, source_target_pairs={{0,240},{1,241},{2,242},{3,243},{4,244},{5,245},{6,246},{7,247},{8... | collective-permute-start | bytes 6152 | tf_op jit(solution)/shard_map/ppermute | solution.py:17
  706.7 27.9 %collective-permute-start.53 = (f32[8,64]{0,1:T(8,128)S(1)}, f32[8,64]{0,1:T(8,128)S(1)}, u32[]{:S(2)}, u32[]{:S(2)}) collective-permute-start(f32[8,64]{0,1:T(8,128)S(1)} %get-tuple-element.37), channel_id=1, source_target_pairs={{0,16},{1,17},{2,18},{3,19},{4,20},{5,21},{6,22},{7,23},{8,24},{9,... | collective-permute-start | bytes 6152 | tf_op jit(solution)/shard_map/ppermute | solution.py:17
  712.1 51.0 %collective-permute-start.60 = (f32[1,32]{1,0:T(1,128)}, f32[1,32]{1,0:T(1,128)}, u32[]{:S(2)}, u32[]{:S(2)}) collective-permute-start(f32[1,32]{1,0:T(1,128)} %get-tuple-element.105), channel_id=1, source_target_pairs={{0,255},{1,0},{2,1},{3,2},{4,3},{5,4},{6,5},{7,6},{8,7},{9,8},{10,... | collective-permute-start | bytes 392 | tf_op jit(solution)/shard_map/ppermute | solution.py:17
  716.5 47.6 %collective-permute-start.61 = (f32[1,32]{1,0:T(1,128)}, f32[1,32]{1,0:T(1,128)}, u32[]{:S(2)}, u32[]{:S(2)}) collective-permute-start(f32[1,32]{1,0:T(1,128)} %get-tuple-element.104), channel_id=1, source_target_pairs={{0,1},{1,2},{2,3},{3,4},{4,5},{5,6},{6,7},{7,8},{8,9},{9,10},{10,1... | collective-permute-start | bytes 392 | tf_op jit(solution)/shard_map/ppermute | solution.py:17
  719.9 46.6 %collective-permute-start.62 = (f32[1,32]{1,0:T(1,128)}, f32[1,32]{1,0:T(1,128)}, u32[]{:S(2)}, u32[]{:S(2)}) collective-permute-start(f32[1,32]{1,0:T(1,128)} %get-tuple-element.103), channel_id=1, source_target_pairs={{0,252},{1,253},{2,254},{3,255},{4,0},{5,1},{6,2},{7,3},{8,4},{9,5... | collective-permute-start | bytes 392 | tf_op jit(solution)/shard_map/ppermute | solution.py:17
  731.6 34.9 %collective-permute-start.63 = (f32[1,32]{1,0:T(1,128)}, f32[1,32]{1,0:T(1,128)}, u32[]{:S(2)}, u32[]{:S(2)}) collective-permute-start(f32[1,32]{1,0:T(1,128)} %get-tuple-element.102), channel_id=1, source_target_pairs={{0,4},{1,5},{2,6},{3,7},{4,8},{5,9},{6,10},{7,11},{8,12},{9,13},{1... | collective-permute-start | bytes 392 | tf_op jit(solution)/shard_map/ppermute | solution.py:17
  757.1 20.3 %collective-permute-start.54 = (f32[8,32]{0,1:T(8,128)}, f32[8,32]{0,1:T(8,128)}, u32[]{:S(2)}, u32[]{:S(2)}) collective-permute-start(f32[8,32]{0,1:T(8,128)} %get-tuple-element.72), channel_id=1, source_target_pairs={{0,255},{1,0},{2,1},{3,2},{4,3},{5,4},{6,5},{7,6},{8,7},{9,8},{10,... | collective-permute-start | bytes 3080 | tf_op jit(solution)/shard_map/ppermute | solution.py:17
  766.5 19.3 %collective-permute-start.55 = (f32[8,32]{0,1:T(8,128)}, f32[8,32]{0,1:T(8,128)}, u32[]{:S(2)}, u32[]{:S(2)}) collective-permute-start(f32[8,32]{0,1:T(8,128)} %get-tuple-element.71), channel_id=1, source_target_pairs={{0,1},{1,2},{2,3},{3,4},{4,5},{5,6},{6,7},{7,8},{8,9},{9,10},{10,1... | collective-permute-start | bytes 3080 | tf_op jit(solution)/shard_map/ppermute | solution.py:17
  766.6 21.7 %collective-permute-start.56 = (f32[8,32]{0,1:T(8,128)S(1)}, f32[8,32]{0,1:T(8,128)}, u32[]{:S(2)}, u32[]{:S(2)}) collective-permute-start(f32[8,32]{0,1:T(8,128)S(1)} %get-tuple-element.70), channel_id=1, source_target_pairs={{0,252},{1,253},{2,254},{3,255},{4,0},{5,1},{6,2},{7,3},{8,4},{9,5... | collective-permute-start | bytes 3080 | tf_op jit(solution)/shard_map/ppermute | solution.py:17
  777.5 18.2 %collective-permute-start.59 = (f32[8,32]{0,1:T(8,128)S(1)}, f32[8,32]{0,1:T(8,128)}, u32[]{:S(2)}, u32[]{:S(2)}) collective-permute-start(f32[8,32]{0,1:T(8,128)S(1)} %get-tuple-element.67), channel_id=1, source_target_pairs={{0,16},{1,17},{2,18},{3,19},{4,20},{5,21},{6,22},{7,23},{8,24},{9,... | collective-permute-start | bytes 3080 | tf_op jit(solution)/shard_map/ppermute | solution.py:17
  802.1 32.9 %collective-permute-start.66 = (f32[8,32]{0,1:T(8,128)}, f32[8,32]{0,1:T(8,128)S(1)}, u32[]{:S(2)}, u32[]{:S(2)}) collective-permute-start(f32[8,32]{0,1:T(8,128)} %bitcast.112), channel_id=1, source_target_pairs={{0,1},{1,2},{2,3},{3,4},{4,5},{5,6},{6,7},{7,8},{8,9},{9,10},{10,1... | collective-permute-start | bytes 3080 | tf_op jit(solution)/shard_map/ppermute | solution.py:17
  815.2 25.1 %collective-permute-start.67 = (f32[8,32]{0,1:T(8,128)}, f32[8,32]{0,1:T(8,128)}, u32[]{:S(2)}, u32[]{:S(2)}) collective-permute-start(f32[8,32]{0,1:T(8,128)} %bitcast.113), channel_id=1, source_target_pairs={{0,255},{1,0},{2,1},{3,2},{4,3},{5,4},{6,5},{7,6},{8,7},{9,8},{10,... | collective-permute-start | bytes 3080 | tf_op jit(solution)/shard_map/ppermute | solution.py:17
  817.4 23.6 %collective-permute-start.68 = (f32[8,32]{0,1:T(8,128)}, f32[8,32]{0,1:T(8,128)S(1)}, u32[]{:S(2)}, u32[]{:S(2)}) collective-permute-start(f32[8,32]{0,1:T(8,128)} %bitcast.114), channel_id=1, source_target_pairs={{0,4},{1,5},{2,6},{3,7},{4,8},{5,9},{6,10},{7,11},{8,12},{9,13},{1... | collective-permute-start | bytes 3080 | tf_op jit(solution)/shard_map/ppermute | solution.py:17
  819.6 21.4 %collective-permute-start.69 = (f32[8,32]{0,1:T(8,128)}, f32[8,32]{0,1:T(8,128)S(1)}, u32[]{:S(2)}, u32[]{:S(2)}) collective-permute-start(f32[8,32]{0,1:T(8,128)} %bitcast.115), channel_id=1, source_target_pairs={{0,252},{1,253},{2,254},{3,255},{4,0},{5,1},{6,2},{7,3},{8,4},{9,5... | collective-permute-start | bytes 3080 | tf_op jit(solution)/shard_map/ppermute | solution.py:17
  874.8 19.3 %collective-permute-start.72 = (f32[8,32]{0,1:T(8,128)S(1)}, f32[8,32]{0,1:T(8,128)S(1)}, u32[]{:S(2)}, u32[]{:S(2)}) collective-permute-start(f32[8,32]{0,1:T(8,128)S(1)} %get-tuple-element.66), channel_id=1, source_target_pairs={{0,255},{1,0},{2,1},{3,2},{4,3},{5,4},{6,5},{7,6},{8,7},{9,8},{10,... | collective-permute-start | bytes 3080 | tf_op jit(solution)/shard_map/ppermute | solution.py:17
  888.8 16.5 %collective-permute-start.76 = (f32[8,32]{0,1:T(8,128)S(1)}, f32[8,32]{0,1:T(8,128)}, u32[]{:S(2)}, u32[]{:S(2)}) collective-permute-start(f32[8,32]{0,1:T(8,128)S(1)} %get-tuple-element.62), channel_id=1, source_target_pairs={{0,240},{1,241},{2,242},{3,243},{4,244},{5,245},{6,246},{7,247},{8... | collective-permute-start | bytes 3080 | tf_op jit(solution)/shard_map/ppermute | solution.py:17
  914.5 20.7 %collective-permute-start.78 = (f32[8,32]{0,1:T(8,128)}, f32[8,32]{0,1:T(8,128)}, u32[]{:S(2)}, u32[]{:S(2)}) collective-permute-start(f32[8,32]{0,1:T(8,128)} %bitcast.128), channel_id=1, source_target_pairs={{0,1},{1,2},{2,3},{3,4},{4,5},{5,6},{6,7},{7,8},{8,9},{9,10},{10,1... | collective-permute-start | bytes 3080 | tf_op jit(solution)/shard_map/ppermute | solution.py:17
  953.8 33.9 %collective-permute-start.84 = (f32[8,64]{0,1:T(8,128)S(1)}, f32[8,64]{0,1:T(8,128)S(1)}, u32[]{:S(2)}, u32[]{:S(2)}) collective-permute-start(f32[8,64]{0,1:T(8,128)S(1)} %bitcast.371), channel_id=1, source_target_pairs={{0,1},{1,2},{2,3},{3,4},{4,5},{5,6},{6,7},{7,8},{8,9},{9,10},{10,1... | collective-permute-start | bytes 6152 | tf_op jit(solution)/shard_map/ppermute | solution.py:17
  972.9 20.4 %collective-permute-start.85 = (f32[8,64]{0,1:T(8,128)}, f32[8,64]{0,1:T(8,128)S(1)}, u32[]{:S(2)}, u32[]{:S(2)}) collective-permute-start(f32[8,64]{0,1:T(8,128)} %bitcast.139), channel_id=1, source_target_pairs={{0,255},{1,0},{2,1},{3,2},{4,3},{5,4},{6,5},{7,6},{8,7},{9,8},{10,... | collective-permute-start | bytes 6152 | tf_op jit(solution)/shard_map/ppermute | solution.py:17
  (106 other events, 5222.0 us)
Sparse Core Ops, SparseCore 0:
  1092.0 118.6 all-gather.2
